TPU v7x, 256 devices: a whole 4x4x8 slice. The times are simulated.
256 devices in a mesh: seq: 64 (over y, z, core), tp: 4 (over x).
Axes of the slice: x: 4, y: 4, z: 8, core: 2. Of those that a mesh axis runs over, the one named last changes fastest.
Arguments:
- queries: bfloat16 [98304, 2048], P('seq', 'tp'), may hold values from -160 to 160
- cotangent: bfloat16 [98304, 2048], P('seq', 'tp'), may hold values from -6 to 6
- owner_map: int32 [1536, 1], P('seq'), may hold values from 0 to 63; in each aligned block of 24 rows (0 to 23, 24 to 47, ...) at most 2 rows name the same one
- neighbour_ids: int32 [1536, 2], P('seq'), may hold values from 0 to 1
- database: bfloat16 [128, 128, 1536], P('seq', None, 'tp'), may hold values from -6 to 6
- norm_gain: float32 [1536], P('tp'), may hold values from 0.5 to 2
- key_weight: bfloat16 [1536, 2048], P(None, 'tp'), may hold values from -0.15625 to 0.15625
- value_weight: bfloat16 [1536, 2048], P(None, 'tp'), may hold values from -0.15625 to 0.15625
Outputs:
- attended: bfloat16 [98304, 2048], P('seq', 'tp')
- grad_key_weight: float32 [1536, 2048], P('seq', 'tp')
Inputs may be any that keep to these rules, and one draw needn't show every extreme that they name: `owner_map`: in each aligned block of 24 spans (the spans of one index of seq) no owner is named more than 2 times, a bound that some block reaches.
All inputs are finite; a program needn't handle non-finite values.
Results may differ from a plain program's by a relative error of at most 0.01.
The roundings to bfloat16 on the way count: a program that leaves them out, or rounds other values in their place, can miss the bound.
Values may be sent and summed in bfloat16 or wider, within the bound.
No kernel may reach another device: no remote copies, remote signals or barrier semaphores. Data moves between devices by JAX's collectives and lax.ppermute only.
A program may use at most 128 MiB of HBM per device.

v0:
```python
import math

import jax
import jax.numpy as jnp
from jax import lax
from jax.sharding import PartitionSpec as P

D_HEAD = 128
SPAN = 64


epsilon = 1e-06


def slot_tables(owner_map, neighbour_ids, slot_count, capacity, store_count):
    spans_here = owner_map.shape[0]
    target = owner_map[:, 0]
    matching = (target[:, None] == target[None, :]).astype(jnp.int32)
    span_order = jnp.arange(spans_here)
    earlier = (span_order[None, :] < span_order[:, None]).astype(jnp.int32)
    position = jnp.sum(matching * earlier, axis=1)
    slot_index = target * capacity + position
    placed = (jnp.arange(slot_count)[:, None] == slot_index[None, :]).astype(jnp.bfloat16)
    picked = jnp.sum(
        (neighbour_ids[:, :, None] == jnp.arange(store_count)[None, None, :]).astype(jnp.bfloat16),
        axis=1,
    )
    counts = jnp.dot(placed, picked, preferred_element_type=jnp.float32).astype(jnp.bfloat16)
    return (placed, counts)


def pack_rows(placed, values, groups, capacity):
    spans_here = placed.shape[1]
    flattened = values.reshape(spans_here, -1)
    spread = jnp.dot(placed, flattened, preferred_element_type=jnp.float32).astype(jnp.bfloat16)
    return spread.reshape(groups, capacity, SPAN, values.shape[1])


def project_store(database, norm_gain, key_weight, value_weight):
    floats = database.astype(jnp.float32)
    squares = jnp.sum(floats * floats, axis=2)
    sum_squares = lax.psum(squares, "tp")
    full_width = database.shape[2] * lax.axis_size("tp")
    factor = lax.rsqrt(sum_squares / full_width + epsilon)
    normed_part = (floats * factor[:, :, None] * norm_gain[None, None, :]).astype(jnp.bfloat16)
    normed = lax.all_gather(normed_part, "tp", axis=2, tiled=True)
    normed_rows = normed.reshape(-1, normed.shape[2])
    key_rows = jnp.dot(normed_rows, key_weight, preferred_element_type=jnp.float32).astype(
        jnp.bfloat16
    )
    value_rows = jnp.dot(normed_rows, value_weight, preferred_element_type=jnp.float32).astype(
        jnp.bfloat16
    )
    return (normed_rows, key_rows, value_rows)


def block_weights(query_block, key_rows, multiplicity, inv_root):
    scores = (
        jnp.einsum("sqhd,khd->shqk", query_block, key_rows, preferred_element_type=jnp.float32)
        * inv_root
    )
    present = multiplicity[:, None, None, :] > 0
    masked = jnp.where(present, scores, -jnp.inf)
    highest = jnp.max(masked, axis=3, keepdims=True)
    weights = jnp.where(present, multiplicity[:, None, None, :] * jnp.exp(masked - highest), 0.0)
    return weights / jnp.sum(weights, axis=3, keepdims=True)


def per_device(
    queries, cotangent, owner_map, neighbour_ids, database, norm_gain, key_weight, value_weight
):
    groups = lax.axis_size("seq")
    spans_here = owner_map.shape[0]
    local_width = queries.shape[1]
    heads_here = local_width // D_HEAD
    store_count = database.shape[0]
    stored_len = database.shape[1]
    capacity = max(2, spans_here // groups)
    slot_count = groups * capacity
    block_size = math.gcd(slot_count, max(1, 1024 // SPAN))
    block_count = slot_count // block_size
    inv_root = 1.0 / math.sqrt(D_HEAD)
    placed, counts = slot_tables(owner_map, neighbour_ids, slot_count, capacity, store_count)
    count_send = counts.reshape(groups, capacity, store_count)
    query_send = pack_rows(placed, queries, groups, capacity)
    normed_rows, key_rows, value_rows = project_store(database, norm_gain, key_weight, value_weight)
    key_rows = key_rows.reshape(-1, heads_here, D_HEAD)
    value_rows = value_rows.reshape(-1, heads_here, D_HEAD)

    def blocks_of(received):
        return received.reshape(block_count, block_size, SPAN, heads_here, D_HEAD)

    def attend_rows(probabilities):
        result = jnp.einsum(
            "shqk,khd->sqhd",
            probabilities.astype(jnp.bfloat16),
            value_rows,
            preferred_element_type=jnp.float32,
        )
        return result.astype(jnp.bfloat16)

    def key_terms(probabilities, query_block, cot_block):
        grad_probs = jnp.einsum(
            "sqhd,khd->shqk", cot_block, value_rows, preferred_element_type=jnp.float32
        )
        row_delta = jnp.sum(probabilities * grad_probs, axis=3, keepdims=True)
        grad_scores = (probabilities * (grad_probs - row_delta) * inv_root).astype(jnp.bfloat16)
        return jnp.einsum(
            "shqk,sqhd->khd", grad_scores, query_block, preferred_element_type=jnp.float32
        )

    start = jnp.zeros((store_count * stored_len, heads_here, D_HEAD), jnp.float32)
    query_recv, count_recv = (
        lax.all_to_all(query_send, "seq", split_axis=0, concat_axis=0, tiled=True),
        lax.all_to_all(count_send, "seq", split_axis=0, concat_axis=0, tiled=True),
    )
    count_floats = count_recv.astype(jnp.float32).reshape(slot_count, store_count)
    empty_slot = (jnp.sum(count_floats, axis=1, keepdims=True) == 0).astype(jnp.float32)
    first_column = (jnp.arange(store_count) == 0).astype(jnp.float32)[None, :]
    count_floats = count_floats + empty_slot * first_column
    widened = jnp.repeat(count_floats, stored_len, axis=1)
    multiplicity = widened.reshape(block_count, block_size, store_count * stored_len)

    def forward_block(inputs):
        query_block, count_block = inputs
        return attend_rows(block_weights(query_block, key_rows, count_block, inv_root))

    results = lax.map(forward_block, (blocks_of(query_recv), multiplicity))
    outgoing = results.reshape(groups, capacity, SPAN, local_width)
    back = lax.all_to_all(outgoing, "seq", split_axis=0, concat_axis=0, tiled=True)
    restored = lax.dot_general(
        placed,
        back.reshape(slot_count, -1),
        (((0,), (0,)), ((), ())),
        preferred_element_type=jnp.float32,
    )
    attended = restored.astype(jnp.bfloat16).reshape(-1, local_width)
    cot_send = pack_rows(placed, cotangent, groups, capacity)
    cot_recv = lax.all_to_all(cot_send, "seq", split_axis=0, concat_axis=0, tiled=True)

    def backward_step(running, inputs):
        query_block, cot_block, count_block = inputs
        probabilities = block_weights(query_block, key_rows, count_block, inv_root)
        return (running + key_terms(probabilities, query_block, cot_block), None)

    grad_keys, unused = lax.scan(
        backward_step, start, (blocks_of(query_recv), blocks_of(cot_recv), multiplicity)
    )
    rounded_grad_keys = grad_keys.reshape(store_count * stored_len, local_width).astype(
        jnp.bfloat16
    )
    local_grad = lax.dot_general(
        normed_rows, rounded_grad_keys, (((0,), (0,)), ((), ())), preferred_element_type=jnp.float32
    )
    grad_key_weight = lax.psum_scatter(local_grad, "seq", scatter_dimension=0, tiled=True)
    return (attended, grad_key_weight)


def solution(mesh):
    placed = (
        P("seq", "tp"),
        P("seq", "tp"),
        P("seq", None),
        P("seq", None),
        P("seq", None, "tp"),
        P("tp"),
        P(None, "tp"),
        P(None, "tp"),
    )
    return jax.shard_map(
        per_device,
        mesh=mesh,
        in_specs=placed,
        out_specs=(P("seq", "tp"), P("seq", "tp")),
        check_vma=False,
    )
```

profile of v0, /device:TPU:2, one launch (start us, length us, event | category | flops | bytes accessed | tf_op | source)
XLA Modules:
  0.0 786.3 jit_solution(16184139487565297073)
XLA Ops:
  10.5 12.1 %all-to-all-start = ((bf16[64,2,2]{1,2,0:T(2,128)(2,1)}), bf16[64,2,2]{1,2,0:T(2,128)(2,1)S(1)}, u32[]{:S(2)}, u32[]{:S(2)}) async-start(bf16[64,2,2]{1,2,0:T(2,128)(2,1)} %copy.38), calls=%async_computation | async-start | bytes 65536 | tf_op jit(solution)/shard_map/all_to_all | solution.py:115
  30.7 10.1 %copy.60 = bf16[16,8,64,512]{3,2,1,0:T(8,128)(2,1)} copy(bf16[16,8,64,512]{3,1,2,0:T(8,128)(2,1)} %bitcast.175) | data formatting | bytes 16777216
  40.9 11.1 %all-to-all-start.1 = ((bf16[64,2,64,512]{3,2,1,0:T(8,128)(2,1)}), bf16[64,2,64,512]{3,2,1,0:T(8,128)(2,1)}, u32[]{:S(2)}, u32[]{:S(2)}) async-start(bf16[64,2,64,512]{3,2,1,0:T(8,128)(2,1)} %bitcast.173), calls=%async_computation.1 | async-start | bytes 16777216 | tf_op jit(solution)/shard_map/all_to_all | solution.py:114
  60.1 10.2 %copy.62 = bf16[16,8,64,512]{3,2,1,0:T(8,128)(2,1)} copy(bf16[16,8,64,512]{3,1,2,0:T(8,128)(2,1)} %bitcast.176) | data formatting | bytes 16777216
  70.4 8.6 %psum.7 = f32[2,128]{1,0:T(2,128)S(1)} all-reduce(f32[2,128]{1,0:T(2,128)S(1)} %fusion.57), channel_id=1, replica_groups=mesh['seq'=64,'tp'=4] {'tp'}, use_global_device_ids=true, to_apply=%region_4.0 | all-reduce | flops 256 | bytes 2048 | tf_op jit(solution)/shard_map/psum | solution.py:42
  79.1 157.6 %all-to-all-done.1 = bf16[64,2,64,512]{3,2,1,0:T(8,128)(2,1)} async-done(((bf16[64,2,64,512]{3,2,1,0:T(8,128)(2,1)}), bf16[64,2,64,512]{3,2,1,0:T(8,128)(2,1)}, u32[]{:S(2)}, u32[]{:S(2)}) %all-to-all-start.1) | async-done | bytes 8388640 | tf_op jit(solution)/shard_map/all_to_all | solution.py:114
  243.8 14.5 %all_gather.3 = bf16[2,128,1536]{2,1,0:T(8,128)(2,1)S(1)} all-gather(bf16[2,128,384]{2,1,0:T(8,128)(2,1)S(1)} %fusion.59), channel_id=1, replica_groups=mesh['seq'=64,'tp'=4] {'tp'}, dimensions={2}, use_global_device_ids=true | all-gather | bytes 983040 | tf_op jit(solution)/shard_map/all_gather | solution.py:46
  261.9 12.5 %reshape.107 = bf16[8,16,64,4,128]{4,3,2,1,0:T(4,128)(2,1)} reshape(bf16[64,2,64,512]{3,2,1,0:T(8,128)(2,1)} %all-to-all-done.1) | data formatting | bytes 16777216 | tf_op jit(solution)/shard_map/reshape | solution.py:91
  274.4 8.9 %copy.41 = bf16[8,16,64,4,128]{4,2,1,3,0:T(8,128)(2,1)} copy(bf16[8,16,64,4,128]{4,3,2,1,0:T(4,128)(2,1)} %reshape.107) | data formatting | bytes 16777216 | tf_op jit(solution)/shard_map/while | solution.py:128
  283.3 67.3 %while.21 = (s32[]{:T(128)}, bf16[8,16,64,4,128]{4,3,2,1,0:T(4,128)(2,1)}, f32[8,16,256]{2,1,0:T(8,128)S(1)}, bf16[8,16,64,4,128]{4,2,1,3,0:T(8,128)(2,1)}, bf16...) while((s32[]{:T(128)}, bf16[8,16,64,4,128]{4,3,2,1,0:T(4,128)(2,1)}, ...), condition=%wide.region_8.9_spmd, body=%wide.region_5.8_spmd.sunk | while | flops 547885312 | bytes 21587024 | solution.py:128
  350.6 13.1 %reshape.111 = bf16[64,2,64,512]{3,2,1,0:T(8,128)(2,1)} reshape(bf16[8,16,64,4,128]{4,3,2,1,0:T(4,128)(2,1)} %get-tuple-element.71) | data formatting | bytes 16777216 | tf_op jit(solution)/shard_map/reshape | solution.py:129
  363.7 65.0 %all-to-all-done.3 = bf16[64,2,64,512]{3,2,1,0:T(8,128)(2,1)} async-done(((bf16[64,2,64,512]{3,2,1,0:T(8,128)(2,1)}), bf16[64,2,64,512]{3,2,1,0:T(8,128)(2,1)}, u32[]{:S(2)}, u32[]{:S(2)}) %all-to-all-start.3) | async-done | bytes 8388640 | tf_op jit(solution)/shard_map/all_to_all | solution.py:139
  435.7 12.6 %reshape.116 = bf16[8,16,64,4,128]{4,3,2,1,0:T(4,128)(2,1)} reshape(bf16[64,2,64,512]{3,2,1,0:T(8,128)(2,1)} %all-to-all-done.3) | data formatting | bytes 16777216 | tf_op jit(solution)/shard_map/reshape | solution.py:91
  448.3 184.9 %while.22 = (s32[]{:T(128)}, f32[256,4,128]{0,2,1:T(8,128)S(1)}, bf16[8,16,64,4,128]{4,2,1,3,0:T(8,128)(2,1)}, f32[8,16,256]{2,1,0:T(8,128)S(1)}, bf16[256,4,128...) while((s32[]{:T(128)}, f32[256,4,128]{0,2,1:T(8,128)S(1)}, ...), condition=%wide.region_13.14_spmd.clone, body=%wide.region_9.13_spmd.clone.sunk | while | flops 819217152 | bytes 40428652 | solution.py:146
  463.8 7.6 fusion.108
  486.9 7.6 fusion.108
  510.0 7.6 fusion.108
  533.1 7.6 fusion.108
  556.2 7.6 fusion.108
  579.3 7.6 fusion.108
  602.4 7.6 fusion.108
  625.4 7.6 fusion.108
  635.7 12.4 %copy.61 = bf16[16,8,64,512]{3,1,2,0:T(8,128)(2,1)} copy(bf16[16,8,64,512]{3,2,1,0:T(8,128)(2,1)} %bitcast.41) | data formatting | bytes 16777216
  655.1 124.1 %reduce-scatter.2.cloned.1.call-done = f32[24,512]{1,0:T(8,128)} async-done(((f32[1536,512]{1,0:T(8,128)}), f32[24,512]{1,0:T(8,128)}) %reduce-scatter.2.cloned.1.call-update) | async-done | bytes 49168 | tf_op jit(solution)/shard_map/reduce_scatter | solution.py:155
  (132 shorter events, 237.8 us)
Async XLA Ops:
  7.2 251.2 %copy-start = (bf16[1536,512]{1,0:T(8,128)(2,1)S(1)}, bf16[1536,512]{1,0:T(8,128)(2,1)}, u32[]{:S(2)}) copy-start(bf16[1536,512]{1,0:T(8,128)(2,1)} %param.18) | copy-start | bytes 4718596
  8.8 45.7 %copy-start.4 = (s32[24]{0:T(128)}, s32[24]{0:T(128)S(1)}, u32[]{:S(2)}) copy-start(s32[24]{0:T(128)S(1)} %multiply_add_fusion.1) | copy-start | bytes 292
  10.5 30.4 %all-to-all-start = ((bf16[64,2,2]{1,2,0:T(2,128)(2,1)}), bf16[64,2,2]{1,2,0:T(2,128)(2,1)S(1)}, u32[]{:S(2)}, u32[]{:S(2)}) async-start(bf16[64,2,2]{1,2,0:T(2,128)(2,1)} %copy.38), calls=%async_computation | async-start | bytes 65536 | tf_op jit(solution)/shard_map/all_to_all | solution.py:115
  40.9 195.9 %all-to-all-start.1 = ((bf16[64,2,64,512]{3,2,1,0:T(8,128)(2,1)}), bf16[64,2,64,512]{3,2,1,0:T(8,128)(2,1)}, u32[]{:S(2)}, u32[]{:S(2)}) async-start(bf16[64,2,64,512]{3,2,1,0:T(8,128)(2,1)} %bitcast.173), calls=%async_computation.1 | async-start | bytes 16777216 | tf_op jit(solution)/shard_map/all_to_all | solution.py:114
  60.1 10.2 %copy-start.2 = (bf16[2,128,384]{2,1,0:T(8,128)(2,1)S(1)}, bf16[2,128,384]{2,1,0:T(8,128)(2,1)}, u32[]{:S(2)}) copy-start(bf16[2,128,384]{2,1,0:T(8,128)(2,1)} %param.16) | copy-start | bytes 589828
  60.1 18.9 %copy-start.6 = (f32[384]{0:T(512)S(1)}, f32[384]{0:T(512)}, u32[]{:S(2)}) copy-start(f32[384]{0:T(512)} %param.17) | copy-start | bytes 4612
  236.8 191.9 %all-to-all-start.3 = ((bf16[64,2,64,512]{3,2,1,0:T(8,128)(2,1)}), bf16[64,2,64,512]{3,2,1,0:T(8,128)(2,1)}, u32[]{:S(2)}, u32[]{:S(2)}) async-start(bf16[64,2,64,512]{3,2,1,0:T(8,128)(2,1)} %bitcast.172), calls=%async_computation.3 | async-start | bytes 16777216 | tf_op jit(solution)/shard_map/all_to_all | solution.py:139
  428.7 207.0 %all-to-all-start.2 = ((bf16[64,2,64,512]{3,2,1,0:T(8,128)(2,1)}), bf16[64,2,64,512]{3,2,1,0:T(8,128)(2,1)}, u32[]{:S(2)}, u32[]{:S(2)}) async-start(bf16[64,2,64,512]{3,2,1,0:T(8,128)(2,1)} %reshape.111), calls=%async_computation.2 | async-start | bytes 16777216 | tf_op jit(solution)/shard_map/all_to_all | solution.py:130
  435.7 12.6 %copy-start.3 = (f32[256,4,128]{0,2,1:T(8,128)S(1)}, f32[256,4,128]{0,2,1:T(8,128)}, u32[]{:S(2)}) copy-start(f32[256,4,128]{0,2,1:T(8,128)} %custom-call) | copy-start | bytes 1572868
  435.7 343.5 %reduce-scatter.2.cloned.1.call-start = ((), (), s32[]{:S(2)}) async-start(), calls=%async_computation.5 | async-start | bytes 3194880 | tf_op jit(solution)/shard_map/reduce_scatter | solution.py:155
  635.7 12.5 %copy-start.5 = (s32[24]{0:T(128)S(1)}, s32[24]{0:T(128)}, u32[]{:S(2)}) copy-start(s32[24]{0:T(128)} %copy-done.4) | copy-start | bytes 292
  648.1 131.0 %copy-start.1 = (bf16[1536,512]{1,0:T(8,128)(2,1)S(1)}, bf16[1536,512]{1,0:T(8,128)(2,1)}, u32[]{:S(2)}) copy-start(bf16[1536,512]{1,0:T(8,128)(2,1)} %param.18) | copy-start | bytes 4718596
Sparse Core Ops, SparseCore 0:
  635.8 143.3 reduce-scatter.1
where the time goes:
time: 795 us; the launch traced here: 786 us
  waiting for transfers between devices  347 us (44%)
  matrix products  157 us (20%)
  local copies, waits for them, and re-layouts  117 us (15%)
  other arithmetic  90.1 us (11%)
  starting transfers between devices  37.2 us (5%)
  blocking collectives  23.2 us (3%)
  between operations  14.5 us (2%)
    all_to_all x1, waiting for transfers between devices, per_device(): lax.all_to_all(query_send, 'seq', split_axis=0, concat_axis=0, tiled=True)  158 us
    reduce_scatter x1, waiting for transfers between devices, per_device(): lax.psum_scatter(local_grad, 'seq', scatter_dimension=0, tiled=True)  124 us
    all_to_all x1, waiting for transfers between devices, per_device(): lax.all_to_all(cot_send, 'seq', split_axis=0, concat_axis=0, tiled=True)  65 us
    dot_general x8, matrix products, key_terms(): jnp.einsum('shqk,sqhd->khd', grad_scores, query_block, preferred_element_...  60.5 us
    div x8, other arithmetic, block_weights(): return weights / jnp.sum(weights, axis=3, keepdims=True)  58.8 us
    dot_general x16, matrix products, block_weights(): jnp.einsum('sqhd,khd->shqk', query_block, key_rows, preferred_element_typ...  46.5 us
    unnamed x17, local copies, waits for them, and re-layouts  32.8 us
    sub x8, other arithmetic, block_weights(): masked - highest  28.4 us
  transfers between devices with their start and end apart: 5, of which 3 were waited for; matrix products, arithmetic and copies ran while one was open for 46% of the time, Pallas kernels for 0%

commit v1 on v0

v1 whole, which is shorter than its diff:
```python
import functools
import math

import jax
import jax.numpy as jnp
from jax import lax
from jax.experimental import pallas as pl
from jax.experimental.pallas import tpu as pltpu
from jax.sharding import PartitionSpec as P

D_HEAD = 128
SPAN = 64
NLEN = 128
N_Y, N_Z = 4, 8
CHIPS = N_Y * N_Z
SLOTS = 4
CHUNKS = 2
epsilon = 1e-06


def seq_of(y, z, core):
    return ((y % N_Y) * N_Z + z % N_Z) * 2 + core


PAIR = [(i, i ^ 1) for i in range(2 * CHIPS)]
SAME_CORE = [[seq_of(y, z, c) for y in range(N_Y) for z in range(N_Z)] for c in range(2)]
Z_GROUPS = [[seq_of(y, z, c) for z in range(N_Z)] for y in range(N_Y) for c in range(2)]
Y_GROUPS = [[seq_of(y, z, c) for y in range(N_Y)] for z in range(N_Z) for c in range(2)]


def swap(x):
    return lax.ppermute(x, "seq", PAIR)


def gather_chips(x):
    return lax.all_gather(x, "seq", axis_index_groups=SAME_CORE, axis=0, tiled=False)


def scatter_chips(x):
    rest = x.shape[1:]
    x = x.reshape(N_Y, N_Z * rest[0], *rest[1:])
    x = lax.psum_scatter(x, "seq", axis_index_groups=Y_GROUPS, scatter_dimension=0, tiled=False)
    x = x.reshape(N_Z, *rest)
    return lax.psum_scatter(x, "seq", axis_index_groups=Z_GROUPS, scatter_dimension=0, tiled=False)


def tables(owners, core):
    spans = owners.shape[0]
    order = jnp.arange(spans)
    same = owners[:, None] == owners[None, :]
    position = jnp.sum((same & (order[None, :] < order[:, None])).astype(jnp.int32), axis=1)
    wanted = 2 * jnp.arange(CHIPS) + core
    match = (wanted[:, None] == owners[None, :])[:, None, :] & (
        position[None, None, :] == jnp.arange(SLOTS)[None, :, None]
    )
    slot = jnp.sum(jnp.where(match, order[None, None, :], 0), axis=2)
    count = jnp.sum(match.astype(jnp.int32), axis=(1, 2))
    return count.astype(jnp.int32), slot.reshape(-1).astype(jnp.int32)


def attention_kernel(heads, count, slot, ids, q_ref, cot_ref, kv_ref, att_ref, grad_ref, acc):
    owner = pl.program_id(0)
    inv_root = 1.0 / math.sqrt(D_HEAD)
    acc[...] = jnp.zeros_like(acc)
    first_half = lax.broadcasted_iota(jnp.int32, (1, 2 * NLEN), 1) < NLEN

    def one_span(k, carry):
        span = slot[owner * SLOTS + k]
        rows = pl.ds(pl.multiple_of(span * SPAN, SPAN), SPAN)
        one, two = ids[2 * span], ids[2 * span + 1]
        low = jnp.where((one == 0) | (two == 0), 0.0, -1e30)
        high = jnp.where((one == 1) | (two == 1), 0.0, -1e30)
        bias = jnp.where(first_half, low, high)
        for h in range(heads):
            cols = slice(h * D_HEAD, (h + 1) * D_HEAD)
            q = q_ref[rows, cols]
            cot = cot_ref[rows, cols]
            key = kv_ref[0, :, cols]
            value = kv_ref[0, :, (heads + h) * D_HEAD : (heads + h + 1) * D_HEAD]
            scores = lax.dot_general(
                q, key, (((1,), (1,)), ((), ())), preferred_element_type=jnp.float32
            )
            scores = scores * (inv_root * math.log2(math.e)) + bias
            weights = jnp.exp2(scores - jnp.max(scores, axis=1, keepdims=True))
            probs = weights * (1.0 / jnp.sum(weights, axis=1, keepdims=True))
            att = jnp.dot(probs.astype(jnp.bfloat16), value, preferred_element_type=jnp.float32)
            att_ref[rows, cols] = att.astype(jnp.bfloat16)
            grad_probs = lax.dot_general(
                cot, value, (((1,), (1,)), ((), ())), preferred_element_type=jnp.float32
            )
            delta = jnp.sum(probs * grad_probs, axis=1, keepdims=True)
            grad_scores = (probs * (grad_probs - delta) * inv_root).astype(jnp.bfloat16)
            acc[h] += lax.dot_general(
                q, grad_scores, (((0,), (0,)), ((), ())), preferred_element_type=jnp.float32
            )
        return carry

    lax.fori_loop(0, count[owner], one_span, 0)
    grad_ref[0] = acc[...].reshape(heads * D_HEAD, 2 * NLEN).astype(jnp.bfloat16)


def attend(count, slot, ids, q, cot, kv, chunk):
    heads = kv.shape[2] // (2 * D_HEAD)
    width = heads * D_HEAD
    rows = q.shape[0]
    seen = kv.shape[1]
    return pl.pallas_call(
        functools.partial(attention_kernel, heads),
        grid_spec=pltpu.PrefetchScalarGridSpec(
            num_scalar_prefetch=3,
            grid=(CHIPS,),
            in_specs=[
                pl.BlockSpec((rows, width), lambda o, *_: (0, chunk)),
                pl.BlockSpec((rows, width), lambda o, *_: (0, chunk)),
                pl.BlockSpec((1, seen, 2 * width), lambda o, *_: (o, 0, 0)),
            ],
            out_specs=[
                pl.BlockSpec((rows, width), lambda o, *_: (0, 0)),
                pl.BlockSpec((1, width, seen), lambda o, *_: (o, 0, 0)),
            ],
            scratch_shapes=[pltpu.VMEM((heads, D_HEAD, seen), jnp.float32)],
        ),
        out_shape=[
            jax.ShapeDtypeStruct((rows, width), jnp.bfloat16),
            jax.ShapeDtypeStruct((CHIPS, width, seen), jnp.bfloat16),
        ],
        compiler_params=pltpu.CompilerParams(vmem_limit_bytes=40 * 1024 * 1024),
        cost_estimate=pl.CostEstimate(
            flops=rows * seen * width * 4, bytes_accessed=12 * 1024 * 1024, transcendentals=rows * seen * heads
        ),
    )(count, slot, ids, q, cot, kv)


def normed_store(database, norm_gain):
    rows = database.reshape(-1, database.shape[2])
    stored = rows.shape[0]
    top = lax.reduce_precision(norm_gain, 8, 7)
    middle = lax.reduce_precision(norm_gain - top, 8, 7)
    bottom = norm_gain - top - middle
    gains = jnp.stack([top, middle, bottom]).astype(jnp.bfloat16)
    packed = jnp.concatenate([rows, jnp.pad(gains, ((0, 13), (0, 0)))], axis=0)
    whole = lax.all_gather(packed, "tp", axis=1, tiled=True).astype(jnp.float32)
    floats = whole[:stored]
    gain = whole[stored] + whole[stored + 1] + whole[stored + 2]
    mean = jnp.sum(floats * floats, axis=1, keepdims=True) / floats.shape[1]
    return (floats * lax.rsqrt(mean + epsilon) * gain[None, :]).astype(jnp.bfloat16)


def scatter_gradient(grad):
    width = grad.shape[1]
    core = lax.axis_index("seq") % 2
    parts = grad.reshape(CHIPS, 2, -1, width)
    mine = lax.dynamic_index_in_dim(parts, core, 1, keepdims=False)
    other = lax.dynamic_index_in_dim(parts, 1 - core, 1, keepdims=False)
    total = mine + swap(other.astype(jnp.bfloat16)).astype(jnp.float32)
    for groups in (Y_GROUPS, Z_GROUPS):
        size = len(groups[0])
        total = total.astype(jnp.bfloat16).reshape(size, -1, parts.shape[2], width)
        total = lax.all_to_all(total, "seq", 0, 0, axis_index_groups=groups, tiled=True)
        total = jnp.sum(total.astype(jnp.float32), axis=0)
    return total.reshape(parts.shape[2], width)


def per_device(
    queries, cotangent, owner_map, neighbour_ids, database, norm_gain, key_weight, value_weight
):
    core = lax.axis_index("seq") % 2
    tokens, local_width = queries.shape
    width = local_width // CHUNKS

    meta = jnp.concatenate([owner_map, neighbour_ids], axis=1)
    meta = jnp.concatenate([meta, swap(meta)], axis=0)
    q = jnp.concatenate([queries, swap(queries)], axis=0)
    cot = jnp.concatenate([cotangent, swap(cotangent)], axis=0)
    owners, ids = meta[:, 0], meta[:, 1:].reshape(-1)
    count, slot = tables(owners, core)

    normed = normed_store(database, norm_gain)
    key_rows = jnp.dot(normed, key_weight, preferred_element_type=jnp.float32).astype(jnp.bfloat16)
    value_rows = jnp.dot(normed, value_weight, preferred_element_type=jnp.float32).astype(
        jnp.bfloat16
    )

    here = (owner_map % 2) == core
    here = jnp.broadcast_to(here, (here.shape[0], SPAN)).reshape(tokens, 1)
    attended, grads = [], []
    for chunk in range(CHUNKS):
        cols = slice(chunk * width, (chunk + 1) * width)
        kv = jnp.concatenate([key_rows[:, cols], value_rows[:, cols]], axis=1)
        kv = gather_chips(kv)
        att, grad_keys = attend(count, slot, ids, q, cot, kv, chunk)
        attended.append(jnp.where(here, att[:tokens], swap(att[tokens:])))
        grad_keys = scatter_chips(grad_keys)
        grad = lax.dot_general(
            normed, grad_keys, (((0,), (1,)), ((), ())), preferred_element_type=jnp.float32
        )
        grads.append(scatter_gradient(grad))
    return jnp.concatenate(attended, axis=1), jnp.concatenate(grads, axis=1)


def solution(mesh):
    placed = (
        P("seq", "tp"),
        P("seq", "tp"),
        P("seq", None),
        P("seq", None),
        P("seq", None, "tp"),
        P("tp"),
        P(None, "tp"),
        P(None, "tp"),
    )
    return jax.shard_map(
        per_device,
        mesh=mesh,
        in_specs=placed,
        out_specs=(P("seq", "tp"), P("seq", "tp")),
        check_vma=False,
    )
```

time: 795 us -> 478 us (0.60)
  matrix products: 157 us -> 4.32 us
  Pallas kernels: 0 us -> 83.7 us
  local copies, waits for them, and re-layouts: 117 us -> 33.7 us
  other arithmetic: 90.1 us -> 19.3 us
  waiting for transfers between devices: 347 us -> 287 us
  starting transfers between devices: 37.2 us -> 17.1 us
    all_to_all x4, waiting for transfers between devices: 223 us -> 22.8 us  [scatter_gradient(): lax.all_to_all(total, 'seq', 0, 0, axis_index_groups=groups, tiled=True)]
    dot_general x47 -> x4, matrix products: 157 us -> 4.32 us  [the longest x2 3.1 us: per_device(): lax.dot_general(normed, grad_keys, (((0,), (1,)), ((), ())), preferred_el...]
    all_gather x0 -> x2, waiting for transfers between devices: none -> 140 us  [gather_chips(): lax.all_gather(x, 'seq', axis_index_groups=SAME_CORE, axis=0, tiled=False)]
    pallas_call x0 -> x2, Pallas kernels: none -> 83.7 us  [attend(): pl.pallas_call(functools.partial(attention_kernel, heads), grid_spec=pltp...]
    div x8 -> x0, other arithmetic: 58.8 us -> none  [block_weights(): return weights / jnp.sum(weights, axis=3, keepdims=True)]
    reshape x9 -> x2, local copies, waits for them, and re-layouts: 46.4 us -> 0.23 us  [the longest x1 0.12 us: per_device(): owners, ids = (meta[:, 0], meta[:, 1:].reshape(-1))]
    sub x8 -> x0, other arithmetic: 28.4 us -> none  [block_weights(): masked - highest]
    all_to_all x4, starting transfers between devices: 37.2 us -> 15.7 us  [scatter_gradient(): lax.all_to_all(total, 'seq', 0, 0, axis_index_groups=groups, tiled=True)]
  transfers between devices with their start and end apart: 5 -> 17, of which waited for: 3 -> 10; matrix products, arithmetic and copies ran while one was open for 46% -> 7% of each run, Pallas kernels for 0% -> 18%
where the time goes in v1:
time: 478 us; the launch traced here: 475 us
  waiting for transfers between devices  287 us (60%)
  Pallas kernels  83.7 us (18%)
  local copies, waits for them, and re-layouts  33.7 us (7%)
  other arithmetic  19.3 us (4%)
  starting transfers between devices  17.1 us (4%)
  blocking collectives  15.4 us (3%)
  between operations  14.4 us (3%)
    all_gather x2, waiting for transfers between devices, gather_chips(): lax.all_gather(x, 'seq', axis_index_groups=SAME_CORE, axis=0, tiled=False)  140 us
    pallas_call x2, Pallas kernels, attend(): pl.pallas_call(functools.partial(attention_kernel, heads), grid_spec=pltp...  83.7 us
    reduce_scatter x2, waiting for transfers between devices, scatter_chips(): lax.psum_scatter(x, 'seq', axis_index_groups=Z_GROUPS, scatter_dimension=...  72.2 us
    reduce_scatter x2, waiting for transfers between devices, scatter_chips(): lax.psum_scatter(x, 'seq', axis_index_groups=Y_GROUPS, scatter_dimension=...  51.7 us
    all_to_all x4, waiting for transfers between devices, scatter_gradient(): lax.all_to_all(total, 'seq', 0, 0, axis_index_groups=groups, tiled=True)  22.8 us
    unnamed x42, local copies, waits for them, and re-layouts  21.7 us
    all_to_all x4, starting transfers between devices, scatter_gradient(): lax.all_to_all(total, 'seq', 0, 0, axis_index_groups=groups, tiled=True)  15.7 us
    all_gather x1, blocking collectives, normed_store(): whole = lax.all_gather(packed, 'tp', axis=1, tiled=True).astype(jnp.float32)  15.4 us
  transfers between devices with their start and end apart: 17, of which 10 were waited for; matrix products, arithmetic and copies ran while one was open for 7% of the time, Pallas kernels for 18%

profile of v1, /device:TPU:2, one launch (start us, length us, event | category | flops | bytes accessed | tf_op | source)
XLA Modules:
  0.0 475.1 jit_solution(10432389700602802934)
XLA Ops:
  9.0 15.4 %all_gather.15 = bf16[272,1536]{1,0:T(8,128)(2,1)S(1)} all-gather(bf16[272,384]{1,0:T(8,128)(2,1)S(1)} %pad_maximum_fusion.3), channel_id=1, replica_groups=mesh['seq'=64,'tp'=4] {'tp'}, dimensions={1}, use_global_device_ids=true | all-gather | bytes 1044480 | tf_op jit(solution)/shard_map/all_gather | solution.py:142
  33.9 2.9 constant_dynamic-update-slice_fusion.q_ref
  39.9 89.1 %all-gather.5.cloned.1.call-done = bf16[8192,512]{1,0:T(8,128)(2,1)} async-done(((bf16[256,512]{1,0:T(8,128)(2,1)}), bf16[8192,512]{1,0:T(8,128)(2,1)}) %all-gather.5.cloned.1.call-update) | async-done | bytes 8388624 | tf_op jit(solution)/shard_map/all_gather | solution.py:36
  132.9 41.8 %shard_map.95 = (bf16[3072,256]{1,0:T(8,128)(2,1)S(1)}, bf16[32,256,256]{2,1,0:T(8,128)(2,1)S(1)}) custom-call(s32[32]{0:T(128)S(1)} %get-tuple-element.11.count, s32[128]{0:T(128)S(1)} %reshape.109.slot, s32[96]{0:T(128)S(1)} %reshape.110.ids, bf16[3072,512]{1,0:T(8,128)(2,1)S(1)} %copy-done.5, bf16[3072,512]{1,0:T(8,128)(2,1)S(1)} %copy-done.3, ...), custom_call_target="tpu_custom_call" | custom-call | flops 805306368 | bytes 12582912 | tf_op jit(solution)/shard_map/pallas_call | solution.py:107
  174.7 2.0 copy-done.7
  176.7 50.9 %all-gather.7.cloned.1.call-done = bf16[8192,512]{1,0:T(8,128)(2,1)} async-done(((bf16[256,512]{1,0:T(8,128)(2,1)}), bf16[8192,512]{1,0:T(8,128)(2,1)}) %all-gather.7.cloned.1.call-update) | async-done | bytes 8388624 | tf_op jit(solution)/shard_map/all_gather | solution.py:36
  231.4 41.8 %shard_map.96 = (bf16[3072,256]{1,0:T(8,128)(2,1)S(1)}, bf16[32,256,256]{2,1,0:T(8,128)(2,1)S(1)}) custom-call(s32[32]{0:T(128)S(1)} %get-tuple-element.11.count, s32[128]{0:T(128)S(1)} %reshape.109.slot, s32[96]{0:T(128)S(1)} %reshape.110.ids, bf16[3072,512]{1,0:T(8,128)(2,1)S(1)} %copy-done.6, bf16[3072,512]{1,0:T(8,128)(2,1)S(1)} %copy-done.4, ...), custom_call_target="tpu_custom_call" | custom-call | flops 805306368 | bytes 12582912 | tf_op jit(solution)/shard_map/pallas_call | solution.py:107
  277.0 51.4 %reduce-scatter.9.cloned.1.call-done = bf16[1,2048,256]{2,1,0:T(8,128)(2,1)} async-done(((bf16[4,2048,256]{2,1,0:T(8,128)(2,1)}), bf16[1,2048,256]{2,1,0:T(8,128)(2,1)}) %reduce-scatter.9.cloned.1.call-update) | async-done | bytes 1048592 | tf_op jit(solution)/shard_map/reduce_scatter | solution.py:42
  328.4 2.5 fusion.27
  330.9 2.3 copy.18
  333.2 36.0 %reduce-scatter.7.cloned.1.call-done = bf16[1,256,256]{2,1,0:T(8,128)(2,1)} async-done(((bf16[8,256,256]{2,1,0:T(8,128)(2,1)}), bf16[1,256,256]{2,1,0:T(8,128)(2,1)}) %reduce-scatter.7.cloned.1.call-update) | async-done | bytes 131088 | tf_op jit(solution)/shard_map/reduce_scatter | solution.py:44
  372.7 36.2 %reduce-scatter.11.cloned.1.call-done = bf16[1,256,256]{2,1,0:T(8,128)(2,1)} async-done(((bf16[8,256,256]{2,1,0:T(8,128)(2,1)}), bf16[1,256,256]{2,1,0:T(8,128)(2,1)}) %reduce-scatter.11.cloned.1.call-update) | async-done | bytes 131088 | tf_op jit(solution)/shard_map/reduce_scatter | solution.py:44
  412.4 2.2 slice.55
  417.0 4.3 all-to-all-start
  421.3 2.1 fusion
  423.4 6.7 %all-to-all-done = bf16[4,8,24,256]{3,2,1,0:T(8,128)(2,1)S(1)} async-done(((bf16[4,8,24,256]{3,2,1,0:T(8,128)(2,1)}), bf16[4,8,24,256]{3,2,1,0:T(8,128)(2,1)S(1)}, u32[]{:S(2)}, u32[]{:S(2)}) %all-to-all-start) | async-done | bytes 393248 | tf_op jit(solution)/shard_map/all_to_all | solution.py:159
  430.8 3.5 all-to-all-start.2
  436.2 6.0 %all-to-all-done.2 = bf16[4,8,24,256]{3,2,1,0:T(8,128)(2,1)S(1)} async-done(((bf16[4,8,24,256]{3,2,1,0:T(8,128)(2,1)}), bf16[4,8,24,256]{3,2,1,0:T(8,128)(2,1)S(1)}, u32[]{:S(2)}, u32[]{:S(2)}) %all-to-all-start.2) | async-done | bytes 393248 | tf_op jit(solution)/shard_map/all_to_all | solution.py:159
  442.2 4.5 all-to-all-start.1
  446.7 3.1 slice_select_fusion.1
  450.5 5.0 %all-to-all-done.1 = bf16[8,1,24,256]{3,2,1,0:T(8,128)(2,1)} async-done(((bf16[8,1,24,256]{3,2,1,0:T(8,128)(2,1)}), bf16[8,1,24,256]{3,2,1,0:T(8,128)(2,1)}, u32[]{:S(2)}, u32[]{:S(2)}) %all-to-all-start.1) | async-done | bytes 98336 | tf_op jit(solution)/shard_map/all_to_all | solution.py:159
  455.6 3.4 all-to-all-start.3
  458.9 2.6 pad_maximum_fusion
  462.5 5.1 %all-to-all-done.3 = bf16[8,1,24,256]{3,2,1,0:T(8,128)(2,1)S(1)} async-done(((bf16[8,1,24,256]{3,2,1,0:T(8,128)(2,1)}), bf16[8,1,24,256]{3,2,1,0:T(8,128)(2,1)S(1)}, u32[]{:S(2)}, u32[]{:S(2)}) %all-to-all-start.3) | async-done | bytes 98336 | tf_op jit(solution)/shard_map/all_to_all | solution.py:159
  (111 shorter events, 39.9 us)
Async XLA Ops:
  7.2 17.7 %copy-start = (bf16[1536,512]{1,0:T(8,128)(2,1)S(1)}, bf16[1536,512]{1,0:T(8,128)(2,1)}, u32[]{:S(2)}) copy-start(bf16[1536,512]{1,0:T(8,128)(2,1)} %param.15) | copy-start | bytes 4718596
  7.2 121.9 %all-gather.5.cloned.1.call-start = ((), (), s32[]{:S(2)}) async-start(), calls=%async_computation.12 | async-start | bytes 8650752 | tf_op jit(solution)/shard_map/all_gather | solution.py:36
  28.1 199.5 %all-gather.7.cloned.1.call-start = ((), (), s32[]{:S(2)}) async-start(), calls=%async_computation.13 | async-start | bytes 8650752 | tf_op jit(solution)/shard_map/all_gather | solution.py:36
  28.9 247.8 %reduce-scatter.5.cloned.1.call-start = ((), (), s32[]{:S(2)}) async-start(), calls=%async_computation.8 | async-start | bytes 5242880 | tf_op jit(solution)/shard_map/reduce_scatter | solution.py:42
  28.9 4.0 collective-permute-start
  29.1 4.8 %collective-permute-start.1 = (bf16[1536,512]{1,0:T(8,128)(2,1)S(1)}, bf16[1536,512]{1,0:T(8,128)(2,1)}, u32[]{:S(2)}, u32[]{:S(2)}) collective-permute-start(bf16[1536,512]{1,0:T(8,128)(2,1)S(1)} %copy-done.14), channel_id=1, source_target_pairs={{0,4},{4,0},{8,12},{12,8},{16,20},{20,16},{24,28},{28,24},{32,36},... | collective-permute-start | bytes 4718600 | tf_op jit(solution)/shard_map/ppermute | solution.py:32
  29.5 7.2 %collective-permute-start.2 = (bf16[1536,512]{1,0:T(8,128)(2,1)}, bf16[1536,512]{1,0:T(8,128)(2,1)}, u32[]{:S(2)}, u32[]{:S(2)}) collective-permute-start(bf16[1536,512]{1,0:T(8,128)(2,1)} %param.9), channel_id=1, source_target_pairs={{0,4},{4,0},{8,12},{12,8},{16,20},{20,16},{24,28},{28,24},{32,36},... | collective-permute-start | bytes 4718600 | tf_op jit(solution)/shard_map/ppermute | solution.py:32
  29.7 2.0 copy-start.15
  33.9 2.9 copy-start.1
  174.7 2.0 copy-start.7
  176.7 151.7 %reduce-scatter.9.cloned.1.call-start = ((), (), s32[]{:S(2)}) async-start(), calls=%async_computation.10 | async-start | bytes 5242880 | tf_op jit(solution)/shard_map/reduce_scatter | solution.py:42
  227.6 1.9 copy-start.4
  273.2 1.9 copy-start.8
  276.4 92.8 %reduce-scatter.7.cloned.1.call-start = ((), (), s32[]{:S(2)}) async-start(), calls=%async_computation.9 | async-start | bytes 1179648 | tf_op jit(solution)/shard_map/reduce_scatter | solution.py:44
  276.9 132.0 %reduce-scatter.11.cloned.1.call-start = ((), (), s32[]{:S(2)}) async-start(), calls=%async_computation.11 | async-start | bytes 1179648 | tf_op jit(solution)/shard_map/reduce_scatter | solution.py:44
  372.7 43.4 %collective-permute-start.5 = (bf16[32,24,256]{2,1,0:T(8,128)(2,1)}, bf16[32,24,256]{2,1,0:T(8,128)(2,1)S(1)}, u32[]{:S(2)}, u32[]{:S(2)}) collective-permute-start(bf16[32,24,256]{2,1,0:T(8,128)(2,1)} %fusion.2), channel_id=1, source_target_pairs={{0,4},{4,0},{8,12},{12,8},{16,20},{20,16},{24,28},{28,24},{32,36},... | collective-permute-start | bytes 1179656 | tf_op jit(solution)/shard_map/ppermute | solution.py:32
  412.4 8.9 %collective-permute-start.6 = (bf16[32,24,256]{2,1,0:T(8,128)(2,1)}, bf16[32,24,256]{2,1,0:T(8,128)(2,1)}, u32[]{:S(2)}, u32[]{:S(2)}) collective-permute-start(bf16[32,24,256]{2,1,0:T(8,128)(2,1)} %fusion.3), channel_id=1, source_target_pairs={{0,4},{4,0},{8,12},{12,8},{16,20},{20,16},{24,28},{28,24},{32,36},... | collective-permute-start | bytes 1179656 | tf_op jit(solution)/shard_map/ppermute | solution.py:32
  412.4 3.7 copy-start.13
  414.6 32.1 %collective-permute-start.4 = (bf16[1536,256]{1,0:T(8,128)(2,1)}, bf16[1536,256]{1,0:T(8,128)(2,1)}, u32[]{:S(2)}, u32[]{:S(2)}) collective-permute-start(bf16[1536,256]{1,0:T(8,128)(2,1)} %slice.55), channel_id=1, source_target_pairs={{0,4},{4,0},{8,12},{12,8},{16,20},{20,16},{24,28},{28,24},{32,36},... | collective-permute-start | bytes 2359304 | tf_op jit(solution)/shard_map/ppermute | solution.py:32
  416.1 30.6 %collective-permute-start.3 = (bf16[1536,256]{1,0:T(8,128)(2,1)}, bf16[1536,256]{1,0:T(8,128)(2,1)}, u32[]{:S(2)}, u32[]{:S(2)}) collective-permute-start(bf16[1536,256]{1,0:T(8,128)(2,1)} %slice.51), channel_id=1, source_target_pairs={{0,4},{4,0},{8,12},{12,8},{16,20},{20,16},{24,28},{28,24},{32,36},... | collective-permute-start | bytes 2359304 | tf_op jit(solution)/shard_map/ppermute | solution.py:32
  417.0 13.1 %all-to-all-start = ((bf16[4,8,24,256]{3,2,1,0:T(8,128)(2,1)}), bf16[4,8,24,256]{3,2,1,0:T(8,128)(2,1)S(1)}, u32[]{:S(2)}, u32[]{:S(2)}) async-start(bf16[4,8,24,256]{3,2,1,0:T(8,128)(2,1)} %bitcast.57), calls=%async_computation.2 | async-start | bytes 786432 | tf_op jit(solution)/shard_map/all_to_all | solution.py:159
  430.8 11.4 %all-to-all-start.2 = ((bf16[4,8,24,256]{3,2,1,0:T(8,128)(2,1)}), bf16[4,8,24,256]{3,2,1,0:T(8,128)(2,1)S(1)}, u32[]{:S(2)}, u32[]{:S(2)}) async-start(bf16[4,8,24,256]{3,2,1,0:T(8,128)(2,1)} %bitcast.56), calls=%async_computation.6 | async-start | bytes 786432 | tf_op jit(solution)/shard_map/all_to_all | solution.py:159
  442.2 13.4 %all-to-all-start.1 = ((bf16[8,1,24,256]{3,2,1,0:T(8,128)(2,1)}), bf16[8,1,24,256]{3,2,1,0:T(8,128)(2,1)}, u32[]{:S(2)}, u32[]{:S(2)}) async-start(bf16[8,1,24,256]{3,2,1,0:T(8,128)(2,1)} %bitcast.60), calls=%async_computation.3 | async-start | bytes 196608 | tf_op jit(solution)/shard_map/all_to_all | solution.py:159
  455.6 12.0 %all-to-all-start.3 = ((bf16[8,1,24,256]{3,2,1,0:T(8,128)(2,1)}), bf16[8,1,24,256]{3,2,1,0:T(8,128)(2,1)S(1)}, u32[]{:S(2)}, u32[]{:S(2)}) async-start(bf16[8,1,24,256]{3,2,1,0:T(8,128)(2,1)} %bitcast.24), calls=%async_computation.7 | async-start | bytes 196608 | tf_op jit(solution)/shard_map/all_to_all | solution.py:159
  (13 other events, 19.6 us)
Sparse Core Ops, SparseCore 0:
  28.2 100.8 all-gather.4
  131.7 95.9 all-gather.6
  230.2 46.4 reduce-scatter.4
  279.2 49.1 reduce-scatter.8
  330.8 38.3 reduce-scatter.6
  371.6 37.3 reduce-scatter.10
